TPU v7x, 32 devices: a whole 2x2x4 slice. The times are simulated.
32 devices in a mesh: seq: 8 (over y, x, core), tensor: 4 (over z).
Axes of the slice: x: 2, y: 2, z: 4, core: 2. Of those that a mesh axis runs over, the one named last changes fastest.
Arguments:
- hidden: bfloat16 [8192, 3072], P('seq', 'tensor'), may hold values from -6 to 6
- norm_gain: float32 [3072], replicated, may hold values from 0.1 to 1.9
- query_weight: bfloat16 [3072, 4096], P(None, 'tensor'), may hold values from -0.25 to 0.25
- key_weight: bfloat16 [3072, 4096], P(None, 'tensor'), may hold values from -2 to 2
- value_weight: bfloat16 [3072, 4096], P(None, 'tensor'), may hold values from -0.109375 to 0.109375
- output_weight: bfloat16 [4096, 3072], P('tensor'), may hold values from -1.25 to 1.25
- final_gain: float32 [3072], replicated, may hold values from 0.1 to 1.9
- reward_weight: float32 [3072], replicated, may hold values from -6 to 6
- token_ids: int32 [8192], P(('seq', 'tensor')), may hold values from 0 to 255999, as said below
- index_samples: float32 [8, 8, 8192], P(None, None, ('seq', 'tensor')), may hold values from -6 to 6
- feat_weight: float32 [3072, 256], replicated, may hold values from -0.109375 to 0.109375
- index_weight: float32 [8, 256], replicated, may hold values from -2 to 2
- first_bias: float32 [256], replicated, may hold values from -3 to 3
- middle_weight: float32 [256, 256], replicated, may hold values from -0.375 to 0.375
- second_bias: float32 [256], replicated, may hold values from -3 to 3
- head_weight: float32 [256, 8], replicated, may hold values from -0.375 to 0.375
- pair_ids: int32 [8, 2], replicated, may hold values from 0 to 15, all different within a row
Outputs:
- features: bfloat16 [8192, 3072], P(('seq', 'tensor'))
- pair_margin: float32 [8, 8], replicated
- grad_feature: float32 [3072, 256], P(('seq', 'tensor'))
- grad_index: float32 [8, 256], replicated
- grad_first: float32 [256], replicated
- grad_middle: float32 [256, 256], replicated
- grad_second: float32 [256], replicated
- grad_head: float32 [256, 8], replicated
Inputs may be any that keep to these rules, and one draw needn't show every extreme that they name: `token_ids`: in each response of 512 positions the positions before its last valid one hold ids from 2 to 255999, the last valid one holds 1 and the positions after it hold 0; every response has at least 128 valid tokens and at least one 0; the first position of the first response holds 255999. `pair_ids`: each row names two different responses, chosen first; every response stands in exactly one pair.
All inputs are finite; a program needn't handle non-finite values.
Results may differ from a plain program's by a relative error of at most 0.012.
The roundings to bfloat16 on the way count: a program that leaves them out, or rounds other values in their place, can miss the bound.
Values may be sent and summed in bfloat16 or wider, within the bound.
A program may use at most 128 MiB of HBM per device.

v0:
```python
import jax
import jax.numpy as jnp
from jax import lax
from jax.sharding import PartitionSpec as P

HEAD_DIM = 256
RESP_LEN = 512
norm_eps = 1e-06
rope_base = 10000.0
gelu_coef = 0.044715
gelu_root = 0.7978845608028654
masked_score = -1e30


def rms_scale(rows, gain):
    mean_square = jnp.mean(rows * rows, axis=-1, keepdims=True)
    return rows * lax.rsqrt(mean_square + norm_eps) * (1.0 + gain)


def rotate_pairs(entries, positions):
    half_dim = entries.shape[-1] // 2
    freqs = rope_base ** (-(jnp.arange(half_dim, dtype=jnp.float32) * 2.0) / entries.shape[-1])
    angles = positions.astype(jnp.float32)[:, None] * freqs[None, :]
    cosine = jnp.cos(angles)[:, None, :]
    sine = jnp.sin(angles)[:, None, :]
    first_half = entries[..., :half_dim]
    second_half = entries[..., half_dim:]
    return jnp.concatenate(
        [first_half * cosine - second_half * sine, second_half * cosine + first_half * sine],
        axis=-1,
    )


def gelu_tanh(inputs):
    return (
        0.5 * inputs * (1.0 + jnp.tanh(gelu_root * (inputs + gelu_coef * inputs * inputs * inputs)))
    )


def gelu_slope(inputs):
    tangent = jnp.tanh(gelu_root * (inputs + gelu_coef * inputs * inputs * inputs))
    inner_slope = gelu_root * (1.0 + 3.0 * gelu_coef * inputs * inputs)
    return 0.5 * (1.0 + tangent) + 0.5 * inputs * (1.0 - tangent * tangent) * inner_slope


def shards(
    hidden,
    norm_gain,
    query_weight,
    key_weight,
    value_weight,
    output_weight,
    final_gain,
    reward_weight,
    token_ids,
    index_samples,
    feat_weight,
    index_weight,
    first_bias,
    middle_weight,
    second_bias,
    head_weight,
    pair_ids,
):
    tp_count = lax.axis_size("tensor")
    tp_index = lax.axis_index("tensor")
    seq_index = lax.axis_index("seq")
    whole_rows = lax.all_gather(hidden, "tensor", axis=1, tiled=True)
    tok_seq = whole_rows.shape[0]
    width = whole_rows.shape[1]
    local_heads = query_weight.shape[1] // HEAD_DIM
    local_resp = tok_seq // RESP_LEN
    normed = rms_scale(whole_rows.astype(jnp.float32), norm_gain).astype(jnp.bfloat16)
    positions = jnp.arange(RESP_LEN, dtype=jnp.int32)
    causal = positions[None, :] <= positions[:, None]
    head_shape = (local_resp, RESP_LEN, local_heads, HEAD_DIM)
    queries = jnp.dot(normed, query_weight, preferred_element_type=jnp.float32).reshape(head_shape)
    queries = rotate_pairs(queries, positions).astype(jnp.bfloat16)
    key_rows = jnp.dot(normed, key_weight, preferred_element_type=jnp.float32).reshape(head_shape)
    key_rows = rotate_pairs(key_rows, positions).astype(jnp.bfloat16)
    value_rows = (
        jnp.dot(normed, value_weight, preferred_element_type=jnp.float32)
        .astype(jnp.bfloat16)
        .reshape(head_shape)
    )
    scores = jnp.einsum(
        "rqhd,rkhd->rhqk", queries, key_rows, preferred_element_type=jnp.float32
    ) * HEAD_DIM ** (-0.5)
    scores = jnp.where(causal[None, None, :, :], scores, masked_score)
    highest = jnp.max(scores, axis=-1, keepdims=True)
    weights = jnp.exp(scores - highest)
    probs = (weights / jnp.sum(weights, axis=-1, keepdims=True)).astype(jnp.bfloat16)
    attended = jnp.einsum(
        "rhqk,rkhd->rqhd", probs, value_rows, preferred_element_type=jnp.float32
    ).astype(jnp.bfloat16)
    attended = attended.reshape(tok_seq, local_heads * HEAD_DIM)
    partial_out = jnp.dot(attended, output_weight, preferred_element_type=jnp.float32)
    mixed = lax.psum_scatter(partial_out, "tensor", scatter_dimension=1, tiled=True)
    local_width = mixed.shape[1]
    summed = hidden.astype(jnp.float32) + mixed
    square_sums = lax.psum(jnp.sum(summed * summed, axis=1), "tensor")
    gain_part = lax.dynamic_slice_in_dim(final_gain, tp_index * local_width, local_width, 0)
    local_feat = (
        summed * lax.rsqrt(square_sums[:, None] / width + norm_eps) * (1.0 + gain_part)
    ).astype(jnp.bfloat16)
    features = lax.all_to_all(local_feat, "tensor", split_axis=0, concat_axis=1, tiled=True)
    feat32 = features.astype(jnp.float32)
    tok_epi = feat32.shape[0]
    base = jnp.dot(feat32, reward_weight, precision=lax.Precision.HIGHEST)
    feat_part = jnp.dot(feat32, feat_weight, precision=lax.Precision.HIGHEST)
    index_part = jnp.einsum(
        "sit,ie->ste", index_samples, index_weight, precision=lax.Precision.HIGHEST
    )
    first_pre = feat_part[None, :, :] + index_part + first_bias
    first_act = gelu_tanh(first_pre)
    second_pre = (
        jnp.einsum("ste,ef->stf", first_act, middle_weight, precision=lax.Precision.HIGHEST)
        + second_bias
    )
    second_act = gelu_tanh(second_pre)
    head_out = jnp.einsum("ste,ei->sti", second_act, head_weight, precision=lax.Precision.HIGHEST)
    epinet_out = jnp.einsum("sti,sit->st", head_out, index_samples, precision=lax.Precision.HIGHEST)
    resp_total = 2 * pair_ids.shape[0]
    first_token = (seq_index * tp_count + tp_index) * tok_epi
    token_pos = first_token + jnp.arange(tok_epi, dtype=jnp.int32)
    owner = token_pos // RESP_LEN
    slot_ids = jnp.arange(resp_total, dtype=jnp.int32)
    owner_table = (owner[:, None] == slot_ids[None, :]).astype(jnp.float32)
    valid = (token_ids != 0).astype(jnp.float32)
    part_totals = jnp.dot(
        (base[None, :] + epinet_out) * valid[None, :], owner_table, precision=lax.Precision.HIGHEST
    )
    part_counts = jnp.dot(valid, owner_table, precision=lax.Precision.HIGHEST)
    totals, counts = lax.psum((part_totals, part_counts), ("seq", "tensor"))
    means = totals / counts[None, :]
    sign_table = (pair_ids[:, 0:1] == slot_ids[None, :]).astype(jnp.float32) - (
        pair_ids[:, 1:2] == slot_ids[None, :]
    ).astype(jnp.float32)
    margin = jnp.dot(means, sign_table.T, precision=lax.Precision.HIGHEST)
    pair_margin = margin.T
    margin_grad = -jax.nn.sigmoid(-margin)
    mean_grad = jnp.dot(margin_grad, sign_table, precision=lax.Precision.HIGHEST) / counts[None, :]
    reward_grad = (
        jnp.dot(mean_grad, owner_table.T, precision=lax.Precision.HIGHEST) * valid[None, :]
    )
    out_grad = jnp.einsum("st,sit->sti", reward_grad, index_samples)
    grad_head = jnp.einsum("ste,sti->ei", second_act, out_grad, precision=lax.Precision.HIGHEST)
    second_grad = jnp.einsum(
        "sti,ei->ste", out_grad, head_weight, precision=lax.Precision.HIGHEST
    ) * gelu_slope(second_pre)
    grad_second = jnp.sum(second_grad, axis=(0, 1))
    grad_middle = jnp.einsum("ste,stf->ef", first_act, second_grad, precision=lax.Precision.HIGHEST)
    first_grad = jnp.einsum(
        "stf,ef->ste", second_grad, middle_weight, precision=lax.Precision.HIGHEST
    ) * gelu_slope(first_pre)
    grad_first = jnp.sum(first_grad, axis=(0, 1))
    grad_index = jnp.einsum(
        "sit,ste->ie", index_samples, first_grad, precision=lax.Precision.HIGHEST
    )
    feat_grad = jnp.sum(first_grad, axis=0)
    grad_feature = lax.psum_scatter(
        jnp.einsum("td,te->de", feat32, feat_grad, precision=lax.Precision.HIGHEST),
        ("seq", "tensor"),
        scatter_dimension=0,
        tiled=True,
    )
    summed_grads = lax.psum(
        (grad_index, grad_first, grad_middle, grad_second, grad_head), ("seq", "tensor")
    )
    return (
        features,
        pair_margin,
        grad_feature,
        summed_grads[0],
        summed_grads[1],
        summed_grads[2],
        summed_grads[3],
        summed_grads[4],
    )


def solution(mesh):
    return jax.shard_map(
        shards,
        mesh=mesh,
        in_specs=(
            P("seq", "tensor"),
            P(),
            P(None, "tensor"),
            P(None, "tensor"),
            P(None, "tensor"),
            P("tensor", None),
            P(),
            P(),
            P(("seq", "tensor")),
            P(None, None, ("seq", "tensor")),
            P(),
            P(),
            P(),
            P(),
            P(),
            P(),
            P(),
        ),
        out_specs=(
            P(("seq", "tensor"), None),
            P(),
            P(("seq", "tensor"), None),
            P(),
            P(),
            P(),
            P(),
            P(),
        ),
        check_vma=False,
    )
```

profile of v0, /device:TPU:0, one launch (start us, length us, event | category | flops | bytes accessed | tf_op | source)
XLA Modules:
  0.0 796.9 jit_solution(2931273031737406126)
XLA Ops:
  11.2 116.4 %all-gather.2.cloned.1.call-done = bf16[1024,3072]{1,0:T(8,128)(2,1)} async-done(((bf16[1024,768]{1,0:T(8,128)(2,1)}), bf16[1024,3072]{1,0:T(8,128)(2,1)}) %all-gather.2.cloned.1.call-update) | async-done | bytes 6291472 | tf_op jit(solution)/shard_map/all_gather | solution.py:68
  127.7 4.2 fusion.1
  132.3 9.9 %convolution_convert_fusion = bf16[1024,1024]{1,0:T(8,128)(2,1)} fusion(bf16[3072,1024]{1,0:T(8,128)(2,1)} %param.21, bf16[1024,3072]{1,0:T(8,128)(2,1)S(1)} %copy-done.2, f32[3072]{0:T(1024)S(1)} %broadcast_add_fusion, f32[1024]{0:T(1024)S(1)} %add_rsqrt_fusion.1), kind=kOutput, calls=%fused_computation.51 | convolution fusion | flops 6456082432 | bytes 14696448 | tf_op jit(solution)/shard_map/dot_general | solution.py:82
  142.2 4.5 reshape.148
  146.7 12.1 %fusion.86 = f32[1024,1024]{1,0:T(8,128)} fusion(bf16[3072,1024]{1,0:T(8,128)(2,1)} %param.20, bf16[1024,3072]{1,0:T(8,128)(2,1)} %all-gather.2.cloned.1.call-done, f32[3072]{0:T(1024)S(1)} %broadcast_add_fusion, f32[1024]{0:T(1024)S(1)} %add_rsqrt_fusion.1), kind=kOutput, calls=%fused_computation.132 | convolution fusion | flops 6455033856 | bytes 16793600 | tf_op jit(solution)/shard_map/dot_general | solution.py:79
  158.9 5.6 reshape.150
  164.5 12.1 %fusion.88 = f32[1024,1024]{1,0:T(8,128)} fusion(bf16[3072,1024]{1,0:T(8,128)(2,1)} %param.19, bf16[1024,3072]{1,0:T(8,128)(2,1)} %all-gather.2.cloned.1.call-done, f32[3072]{0:T(1024)S(1)} %broadcast_add_fusion, f32[1024]{0:T(1024)S(1)} %add_rsqrt_fusion.1), kind=kOutput, calls=%fused_computation.133 | convolution fusion | flops 6455033856 | bytes 16793600 | tf_op jit(solution)/shard_map/dot_general | solution.py:77
  176.6 5.8 reshape.149
  189.1 5.6 fusion.95
  194.8 6.1 convert_bitcast_fusion
  200.8 4.2 copy.40
  207.2 12.3 %fusion.97 = f32[1024,3072]{1,0:T(8,128)} fusion(bf16[1024,1024]{1,0:T(8,128)(2,1)S(1)} %bitcast.76, bf16[1024,3072]{1,0:T(8,128)(2,1)} %param.22), kind=kOutput, calls=%fused_computation.140 | convolution fusion | flops 6442450944 | bytes 20971520 | tf_op jit(solution)/shard_map/dot_general | solution.py:97
  220.3 209.4 %reduce-scatter.3.cloned.1.call-done = f32[1024,768]{1,0:T(8,128)} async-done(((f32[1024,3072]{1,0:T(8,128)}), f32[1024,768]{1,0:T(8,128)}) %reduce-scatter.3.cloned.1.call-update) | async-done | bytes 3145744 | tf_op jit(solution)/shard_map/reduce_scatter | solution.py:98
  432.6 11.5 %psum.56 = f32[1024]{0:T(1024)S(1)} all-reduce(f32[1024]{0:T(1024)S(1)} %multiply_reduce_fusion), channel_id=1, replica_groups=mesh['seq'=8,'tensor'=4] {'tensor'}, use_global_device_ids=true, to_apply=%region_5.6 | all-reduce | flops 1024 | bytes 8192 | tf_op jit(solution)/shard_map/psum | solution.py:101
  448.0 4.5 all-to-all-start
  453.1 35.0 %all-to-all-done = bf16[4,256,768]{2,1,0:T(8,128)(2,1)} async-done(((bf16[4,256,768]{2,1,0:T(8,128)(2,1)}), bf16[4,256,768]{2,1,0:T(8,128)(2,1)}, u32[]{:S(2)}, u32[]{:S(2)}) %all-to-all-start) | async-done | bytes 1572896 | tf_op jit(solution)/shard_map/all_to_all | solution.py:106
  500.0 38.3 %all-reduce.1 = (f32[8,16]{1,0:T(8,128)S(1)}, f32[16]{0:T(128)S(1)}) all-reduce(f32[8,16]{1,0:T(8,128)S(1)} %fusion.37, f32[16]{0:T(128)S(1)} %convolution_bitcast_fusion.3), channel_id=1, replica_groups=mesh['seq'=8,'tensor'=4] {'seq','tensor'}, use_global_device_ids=true, to_apply=%region_6.7 | all-reduce | flops 144 | bytes 1152 | tf_op jit(solution)/shard_map/psum | solution.py:134
  538.9 4.9 fusion.96
  545.3 4.6 convolution_bitcast_fusion
  549.9 6.6 fusion.91
  556.8 4.8 fusion.100
  566.9 41.8 %all-reduce = (f32[8,256]{1,0:T(8,128)}, f32[256]{0:T(256)}, f32[256]{0:T(256)}, f32[256,8]{0,1:T(8,128)}) all-reduce(f32[8,256]{1,0:T(8,128)S(1)} %convolution_bitcast_fusion.2, f32[256]{0:T(256)S(1)} %get-tuple-element.24, f32[256]{0:T(256)S(1)} %get-tuple-element.51, ...), channel_id=1, replica_groups=mesh['seq'=8,'tensor'=4] {'seq','tensor'}, use_global_device_ids=true, to_apply=%region_10.11 | all-reduce | flops 4608 | bytes 36864 | tf_op jit(solution)/shard_map/psum | solution.py:167
  608.7 73.4 %all-reduce.4.cloned.1.call-done = f32[256,256]{1,0:T(8,128)} async-done(((f32[256,256]{1,0:T(8,128)}), f32[256,256]{1,0:T(8,128)}) %all-reduce.4.cloned.1.call-update) | async-done | bytes 262160 | tf_op jit(solution)/shard_map/psum | solution.py:167
  682.1 106.4 %reduce-scatter.5.cloned.1.call-done = f32[96,256]{1,0:T(8,128)} async-done(((f32[3072,256]{1,0:T(8,128)}), f32[96,256]{1,0:T(8,128)}) %reduce-scatter.5.cloned.1.call-update) | async-done | bytes 98320 | tf_op jit(solution)/shard_map/reduce_scatter | solution.py:161
  (81 shorter events, 42.3 us)
Async XLA Ops:
  7.2 483.8 %copy-start = (f32[3072,256]{1,0:T(8,128)S(1)}, f32[3072,256]{1,0:T(8,128)}, u32[]{:S(2)}) copy-start(f32[3072,256]{1,0:T(8,128)} %param.27) | copy-start | bytes 9437188
  7.2 120.5 %all-gather.2.cloned.1.call-start = ((), (), s32[]{:S(2)}) async-start(), calls=%async_computation.3 | async-start | bytes 7864320 | tf_op jit(solution)/shard_map/all_gather | solution.py:68
  7.9 421.8 %reduce-scatter.3.cloned.1.call-start = ((), (), s32[]{:S(2)}) async-start(), calls=%async_computation.4 | async-start | bytes 15728640 | tf_op jit(solution)/shard_map/reduce_scatter | solution.py:98
  127.7 4.6 copy-start.2
  182.4 4.2 copy-start.6
  189.1 5.6 copy-start.3
  448.0 4.8 copy-start.12
  448.0 5.0 copy-start.13
  448.0 40.0 %all-to-all-start = ((bf16[4,256,768]{2,1,0:T(8,128)(2,1)}), bf16[4,256,768]{2,1,0:T(8,128)(2,1)}, u32[]{:S(2)}, u32[]{:S(2)}) async-start(bf16[4,256,768]{2,1,0:T(8,128)(2,1)} %bitcast.75), calls=%async_computation.1 | async-start | bytes 3145728 | tf_op jit(solution)/shard_map/all_to_all | solution.py:106
  452.5 37.1 %copy-start.9 = (f32[3072]{0:T(1024)S(1)}, f32[3072]{0:T(1024)}, u32[]{:S(2)}) copy-start(f32[3072]{0:T(1024)} %param.24) | copy-start | bytes 36868
  452.5 229.6 %all-reduce.4.cloned.1.call-start = ((), (), s32[]{:S(2)}) async-start(), calls=%async_computation.6 | async-start | bytes 524288 | tf_op jit(solution)/shard_map/psum | solution.py:167
  489.6 3.2 copy-start.1
  491.0 1.8 copy-start.7
  491.0 1.8 copy-start.10
  491.0 1.8 copy-start.11
  492.8 2.0 copy-start.14
  494.8 2.4 copy-start.4
  494.8 2.4 copy-start.15
  494.8 2.4 copy-start.16
  497.2 2.6 copy-start.17
  538.9 6.3 copy-start.5
  543.9 1.4 copy-start.19
  556.6 231.9 %reduce-scatter.5.cloned.1.call-start = ((), (), s32[]{:S(2)}) async-start(), calls=%async_computation.5 | async-start | bytes 3244032 | tf_op jit(solution)/shard_map/reduce_scatter | solution.py:161
  562.3 2.8 copy-start.18
  (1 other events, 1.3 us)
Sparse Core Ops, SparseCore 0:
  9.6 118.0 all-gather.1
  219.6 210.0 reduce-scatter.2
  556.7 125.3 all-reduce.3
  688.0 100.4 reduce-scatter.4
where the time goes:
time: 806 us; the launch traced here: 797 us
  waiting for transfers between devices  541 us (67%)
  blocking collectives  91.6 us (11%)
  matrix products  90.4 us (11%)
  local copies, waits for them, and re-layouts  32.2 us (4%)
  other arithmetic  22 us (3%)
  between operations  14.3 us (2%)
    reduce_scatter x1, waiting for transfers between devices, shards(): lax.psum_scatter(partial_out, 'tensor', scatter_dimension=1, tiled=True)  209 us
    all_gather x1, waiting for transfers between devices, shards(): whole_rows = lax.all_gather(hidden, 'tensor', axis=1, tiled=True)  116 us
    reduce_scatter x1, waiting for transfers between devices, shards(): lax.psum_scatter(jnp.einsum('td,te->de', feat32, feat_grad, precision=lax...  106 us
    psum x1, waiting for transfers between devices, shards(): lax.psum((grad_index, grad_first, grad_middle, grad_second, grad_head), (...  73.4 us
    psum x1, blocking collectives, shards(): lax.psum((grad_index, grad_first, grad_middle, grad_second, grad_head), (...  41.8 us
    psum x1, blocking collectives, shards(): totals, counts = lax.psum((part_totals, part_counts), ('seq', 'tensor'))  38.3 us
    all_to_all x1, waiting for transfers between devices, shards(): lax.all_to_all(local_feat, 'tensor', split_axis=0, concat_axis=1, tiled=T...  35 us
  transfers between devices with their start and end apart: 5, of which 5 were waited for; matrix products, arithmetic and copies ran while one was open for 2% of the time, Pallas kernels for 0%

commit v1 on v0

--- a/solution.py
+++ b/solution.py
@@ -103,7 +103,10 @@
     local_feat = (
         summed * lax.rsqrt(square_sums[:, None] / width + norm_eps) * (1.0 + gain_part)
     ).astype(jnp.bfloat16)
-    features = lax.all_to_all(local_feat, "tensor", split_axis=0, concat_axis=1, tiled=True)
+    size = lax.axis_size("tensor")
+    blocks = jnp.stack(jnp.split(local_feat, size, axis=0), axis=0)
+    blocks = lax.all_to_all(blocks, "tensor", split_axis=0, concat_axis=0)
+    features = jnp.concatenate(blocks, axis=1)
     feat32 = features.astype(jnp.float32)
     tok_epi = feat32.shape[0]
     base = jnp.dot(feat32, reward_weight, precision=lax.Precision.HIGHEST)

time: 806 us -> 809 us (level)
  no operation moved by 1% of the time
where the time goes in v1:
time: 809 us; the launch traced here: 800 us
  waiting for transfers between devices  539 us (67%)
  blocking collectives  91.7 us (11%)
  matrix products  91.4 us (11%)
  local copies, waits for them, and re-layouts  36 us (4%)
  other arithmetic  22.2 us (3%)
  between operations  14.3 us (2%)
    reduce_scatter x1, waiting for transfers between devices, shards(): lax.psum_scatter(partial_out, 'tensor', scatter_dimension=1, tiled=True)  209 us
    all_gather x1, waiting for transfers between devices, shards(): whole_rows = lax.all_gather(hidden, 'tensor', axis=1, tiled=True)  116 us
    reduce_scatter x1, waiting for transfers between devices, shards(): lax.psum_scatter(jnp.einsum('td,te->de', feat32, feat_grad, precision=lax...  106 us
    psum x1, waiting for transfers between devices, shards(): lax.psum((grad_index, grad_first, grad_middle, grad_second, grad_head), (...  71.3 us
    psum x1, blocking collectives, shards(): lax.psum((grad_index, grad_first, grad_middle, grad_second, grad_head), (...  41.9 us
    psum x1, blocking collectives, shards(): totals, counts = lax.psum((part_totals, part_counts), ('seq', 'tensor'))  38.3 us
    all_to_all x1, waiting for transfers between devices, shards(): blocks = lax.all_to_all(blocks, 'tensor', split_axis=0, concat_axis=0)  35.1 us
  transfers between devices with their start and end apart: 5, of which 5 were waited for; matrix products, arithmetic and copies ran while one was open for 2% of the time, Pallas kernels for 0%

profile of v1, /device:TPU:0, one launch (start us, length us, event | category | flops | bytes accessed | tf_op | source)
XLA Modules:
  0.0 799.8 jit_solution(11612607930272050264)
XLA Ops:
  11.2 116.4 %all-gather.2.cloned.1.call-done = bf16[1024,3072]{1,0:T(8,128)(2,1)} async-done(((bf16[1024,768]{1,0:T(8,128)(2,1)}), bf16[1024,3072]{1,0:T(8,128)(2,1)}) %all-gather.2.cloned.1.call-update) | async-done | bytes 6291472 | tf_op jit(solution)/shard_map/all_gather | solution.py:68
  127.7 4.2 fusion.1
  132.3 9.9 %convolution_convert_fusion = bf16[1024,1024]{1,0:T(8,128)(2,1)} fusion(bf16[3072,1024]{1,0:T(8,128)(2,1)} %param.21, bf16[1024,3072]{1,0:T(8,128)(2,1)S(1)} %copy-done.2, f32[3072]{0:T(1024)S(1)} %broadcast_add_fusion, f32[1024]{0:T(1024)S(1)} %add_rsqrt_fusion.1), kind=kOutput, calls=%fused_computation.51 | convolution fusion | flops 6456082432 | bytes 14696448 | tf_op jit(solution)/shard_map/dot_general | solution.py:82
  142.2 4.5 reshape.151
  146.7 12.1 %fusion.86 = f32[1024,1024]{1,0:T(8,128)} fusion(bf16[3072,1024]{1,0:T(8,128)(2,1)} %param.20, bf16[1024,3072]{1,0:T(8,128)(2,1)} %all-gather.2.cloned.1.call-done, f32[3072]{0:T(1024)S(1)} %broadcast_add_fusion, f32[1024]{0:T(1024)S(1)} %add_rsqrt_fusion.1), kind=kOutput, calls=%fused_computation.137 | convolution fusion | flops 6455033856 | bytes 16793600 | tf_op jit(solution)/shard_map/dot_general | solution.py:79
  158.8 5.6 reshape.153
  164.4 12.1 %fusion.88 = f32[1024,1024]{1,0:T(8,128)} fusion(bf16[3072,1024]{1,0:T(8,128)(2,1)} %param.19, bf16[1024,3072]{1,0:T(8,128)(2,1)} %all-gather.2.cloned.1.call-done, f32[3072]{0:T(1024)S(1)} %broadcast_add_fusion, f32[1024]{0:T(1024)S(1)} %add_rsqrt_fusion.1), kind=kOutput, calls=%fused_computation.138 | convolution fusion | flops 6455033856 | bytes 16793600 | tf_op jit(solution)/shard_map/dot_general | solution.py:77
  176.6 5.8 reshape.152
  189.1 5.6 fusion.95
  194.8 6.1 convert_bitcast_fusion
  200.8 4.2 copy.39
  207.1 12.3 %fusion.97 = f32[1024,3072]{1,0:T(8,128)} fusion(bf16[1024,1024]{1,0:T(8,128)(2,1)S(1)} %bitcast.81, bf16[1024,3072]{1,0:T(8,128)(2,1)} %param.22), kind=kOutput, calls=%fused_computation.145 | convolution fusion | flops 6442450944 | bytes 20971520 | tf_op jit(solution)/shard_map/dot_general | solution.py:97
  220.3 209.4 %reduce-scatter.3.cloned.1.call-done = f32[1024,768]{1,0:T(8,128)} async-done(((f32[1024,3072]{1,0:T(8,128)}), f32[1024,768]{1,0:T(8,128)}) %reduce-scatter.3.cloned.1.call-update) | async-done | bytes 3145744 | tf_op jit(solution)/shard_map/reduce_scatter | solution.py:98
  432.5 11.5 %psum.56 = f32[1024]{0:T(1024)S(1)} all-reduce(f32[1024]{0:T(1024)S(1)} %multiply_reduce_fusion), channel_id=1, replica_groups=mesh['seq'=8,'tensor'=4] {'tensor'}, use_global_device_ids=true, to_apply=%region_5.6 | all-reduce | flops 1024 | bytes 8192 | tf_op jit(solution)/shard_map/psum | solution.py:101
  448.3 4.5 all-to-all-start
  453.1 35.1 %all-to-all-done = bf16[4,256,768]{2,1,0:T(8,128)(2,1)} async-done(((bf16[4,256,768]{2,1,0:T(8,128)(2,1)}), bf16[4,256,768]{2,1,0:T(8,128)(2,1)}, u32[]{:S(2)}, u32[]{:S(2)}) %all-to-all-start) | async-done | bytes 1572896 | tf_op jit(solution)/shard_map/all_to_all | solution.py:108
  502.8 38.3 %all-reduce.1 = (f32[8,16]{1,0:T(8,128)S(1)}, f32[16]{0:T(128)S(1)}) all-reduce(f32[8,16]{1,0:T(8,128)S(1)} %fusion.37, f32[16]{0:T(128)S(1)} %convolution_bitcast_fusion.3), channel_id=1, replica_groups=mesh['seq'=8,'tensor'=4] {'seq','tensor'}, use_global_device_ids=true, to_apply=%region_6.7 | all-reduce | flops 144 | bytes 1152 | tf_op jit(solution)/shard_map/psum | solution.py:137
  541.7 4.9 fusion.96
  548.1 4.6 convolution_bitcast_fusion
  552.7 6.6 fusion.91
  559.6 4.5 fusion.100
  571.9 41.9 %all-reduce = (f32[8,256]{1,0:T(8,128)}, f32[256]{0:T(256)}, f32[256]{0:T(256)}, f32[256,8]{0,1:T(8,128)}) all-reduce(f32[8,256]{1,0:T(8,128)S(1)} %convolution_bitcast_fusion.2, f32[256]{0:T(256)S(1)} %get-tuple-element.24, f32[256]{0:T(256)S(1)} %get-tuple-element.55, ...), channel_id=1, replica_groups=mesh['seq'=8,'tensor'=4] {'seq','tensor'}, use_global_device_ids=true, to_apply=%region_10.11 | all-reduce | flops 4608 | bytes 36864 | tf_op jit(solution)/shard_map/psum | solution.py:170
  613.8 71.3 %all-reduce.4.cloned.1.call-done = f32[256,256]{1,0:T(8,128)} async-done(((f32[256,256]{1,0:T(8,128)}), f32[256,256]{1,0:T(8,128)}) %all-reduce.4.cloned.1.call-update) | async-done | bytes 262160 | tf_op jit(solution)/shard_map/psum | solution.py:170
  685.0 106.4 %reduce-scatter.5.cloned.1.call-done = f32[96,256]{1,0:T(8,128)} async-done(((f32[3072,256]{1,0:T(8,128)}), f32[96,256]{1,0:T(8,128)}) %reduce-scatter.5.cloned.1.call-update) | async-done | bytes 98320 | tf_op jit(solution)/shard_map/reduce_scatter | solution.py:164
  (84 shorter events, 47.4 us)
Async XLA Ops:
  7.2 486.1 %copy-start = (f32[3072,256]{1,0:T(8,128)S(1)}, f32[3072,256]{1,0:T(8,128)}, u32[]{:S(2)}) copy-start(f32[3072,256]{1,0:T(8,128)} %param.27) | copy-start | bytes 9437188
  7.2 120.5 %all-gather.2.cloned.1.call-start = ((), (), s32[]{:S(2)}) async-start(), calls=%async_computation.3 | async-start | bytes 7864320 | tf_op jit(solution)/shard_map/all_gather | solution.py:68
  7.9 421.8 %reduce-scatter.3.cloned.1.call-start = ((), (), s32[]{:S(2)}) async-start(), calls=%async_computation.4 | async-start | bytes 15728640 | tf_op jit(solution)/shard_map/reduce_scatter | solution.py:98
  127.7 4.6 copy-start.2
  182.4 4.2 copy-start.6
  189.1 5.6 copy-start.3
  448.3 4.6 copy-start.12
  448.3 4.8 copy-start.13
  448.3 40.0 %all-to-all-start = ((bf16[4,256,768]{2,1,0:T(8,128)(2,1)}), bf16[4,256,768]{2,1,0:T(8,128)(2,1)}, u32[]{:S(2)}, u32[]{:S(2)}) async-start(bf16[4,256,768]{2,1,0:T(8,128)(2,1)} %pad_maximum_fusion), calls=%async_computation.1 | async-start | bytes 3145728 | tf_op jit(solution)/shard_map/all_to_all | solution.py:108
  452.8 38.3 %copy-start.9 = (f32[3072]{0:T(1024)S(1)}, f32[3072]{0:T(1024)}, u32[]{:S(2)}) copy-start(f32[3072]{0:T(1024)} %param.24) | copy-start | bytes 36868
  452.8 232.2 %all-reduce.4.cloned.1.call-start = ((), (), s32[]{:S(2)}) async-start(), calls=%async_computation.6 | async-start | bytes 524288 | tf_op jit(solution)/shard_map/psum | solution.py:170
  491.1 2.3 copy-start.1
  493.3 2.2 copy-start.7
  493.3 2.2 copy-start.10
  493.3 2.2 copy-start.11
  495.6 2.0 copy-start.14
  497.6 2.4 copy-start.4
  497.6 2.4 copy-start.15
  497.6 2.4 copy-start.16
  500.0 2.6 copy-start.17
  541.7 6.3 copy-start.5
  546.7 1.4 copy-start.19
  559.4 232.1 %reduce-scatter.5.cloned.1.call-start = ((), (), s32[]{:S(2)}) async-start(), calls=%async_computation.5 | async-start | bytes 3244032 | tf_op jit(solution)/shard_map/reduce_scatter | solution.py:164
  567.3 2.8 copy-start.18
  (1 other events, 1.3 us)
Sparse Core Ops, SparseCore 0:
  9.6 118.0 all-gather.1
  219.6 210.0 reduce-scatter.2
  559.5 125.5 all-reduce.3
  690.9 100.4 reduce-scatter.4
